TPU v7x, 256 devices: a whole 4x4x8 slice. The times are simulated.
256 devices in a mesh: ctx: 16 (over x, z_lo, core), ep: 16 (over z_hi, y).
Axes of the slice: x: 4, y: 4, z: 8 (z_hi: 4, z_lo: 2; z = z_hi * 2 + z_lo), core: 2. Of those that a mesh axis runs over, the one named last changes fastest.
Arguments:
- queries: bfloat16 [1024, 128, 576], P('ctx', 'ep'), may hold values from -24 to 24
- latents: bfloat16 [4096, 576], P('ctx'), may hold values from -6 to 6
- value_up: bfloat16 [128, 512, 128], P('ep'), may hold values from -0.25 to 0.25
- out_proj: bfloat16 [16384, 7168], P('ep', 'ctx'), may hold values from -0.375 to 0.375
- residual: bfloat16 [1024, 7168], P('ep', 'ctx'), may hold values from -6 to 6
- expert_gate: bfloat16 [16, 7168, 2048], P('ep', None, 'ctx'), may hold values from -0.0625 to 0.0625
- expert_up: bfloat16 [16, 7168, 2048], P('ep', None, 'ctx'), may hold values from -0.0625 to 0.0625
- expert_down: bfloat16 [16, 2048, 7168], P('ep', 'ctx'), may hold values from -0.125 to 0.125
- route_ids: int32 [1024, 8], P('ep'), may hold values from 0 to 15, all different within a row; in each aligned block of 64 rows (0 to 63, 64 to 127, ...) at most 36 rows name the same one
- route_gates: float32 [1024, 8], P('ep'), may hold values from 0.1 to 0.5
Outputs:
- layer_out: bfloat16 [1024, 7168], P('ep', 'ctx')
Inputs may be any that keep to these rules, and one draw needn't show every extreme that they name: `route_ids`: in every aligned block of 64 rows (the rows of one index of ep) no expert is named more than 36 times, a bound that some block reaches.
All inputs are finite; a program needn't handle non-finite values.
Results may differ from a plain program's by a relative error of at most 0.03.
Values may be sent and summed in bfloat16 or wider, within the bound.
No kernel may reach another device: no remote copies, remote signals or barrier semaphores. Data moves between devices by JAX's collectives and lax.ppermute only.
A program may use at most 128 MiB of HBM per device.

v0:
```python
import jax
import jax.numpy as jnp
from jax import lax
from jax.sharding import PartitionSpec as P

NEG = -1e30


def local(
    queries,
    latents,
    value_up,
    out_proj,
    residual,
    expert_gate,
    expert_up,
    expert_down,
    route_ids,
    route_gates,
):
    query_count, head_count, feature_width = queries.shape
    latent_rows = latents.shape[0]
    latent_width = value_up.shape[1]
    value_width = value_up.shape[2]
    scale = (value_width + feature_width - latent_width) ** (-0.5)
    ctx_devices = lax.axis_size("ctx")
    ep_devices = lax.axis_size("ep")
    window = query_count * ctx_devices
    first_pos = latent_rows * ctx_devices - window + lax.axis_index("ctx") * query_count
    query_pos = first_pos + jnp.arange(query_count, dtype=jnp.int32)
    row_pos = jnp.repeat(query_pos, head_count)
    query_rows = queries.reshape(query_count * head_count, feature_width)
    row_count = query_count * head_count
    piece = lax.all_gather(latents, "ctx", axis=0, tiled=True)
    running_max = jnp.full((row_count,), NEG, jnp.float32)
    scores = jnp.einsum("qc,kc->qk", query_rows, piece, preferred_element_type=jnp.float32) * scale
    key_pos = jnp.arange(piece.shape[0], dtype=jnp.int32)
    scores = jnp.where(key_pos[None, :] <= row_pos[:, None], scores, NEG)
    new_max = jnp.maximum(running_max, jnp.max(scores, axis=1))
    raised = jnp.exp(scores - new_max[:, None])
    soft = raised.astype(jnp.bfloat16)
    added = jnp.dot(soft, piece[:, :latent_width], preferred_element_type=jnp.float32)
    total = jnp.sum(raised, axis=1)
    context = (
        (added / total[:, None]).astype(jnp.bfloat16).reshape(query_count, head_count, latent_width)
    )
    head_out = jnp.einsum(
        "thc,hcv->thv", context, value_up, preferred_element_type=jnp.float32
    ).astype(jnp.bfloat16)
    head_out = head_out.reshape(query_count, head_count * value_width)
    spread = jnp.dot(
        lax.all_gather(head_out, "ctx", axis=0, tiled=True),
        out_proj,
        preferred_element_type=jnp.float32,
    )
    attended = lax.psum_scatter(
        spread.astype(jnp.bfloat16), "ep", scatter_dimension=0, tiled=True
    ).astype(jnp.float32)
    moe_input = (residual.astype(jnp.float32) + attended).astype(jnp.bfloat16)
    token_count, pick_count = route_ids.shape
    experts = ep_devices * expert_gate.shape[0]
    capacity = min(
        token_count, token_count * pick_count // experts + token_count * pick_count // (8 * experts)
    )
    flat_routes = route_ids.reshape(token_count * pick_count)
    one_hot = (flat_routes[:, None] == jnp.arange(experts, dtype=jnp.int32)[None, :]).astype(
        jnp.int32
    )
    before = jnp.cumsum(one_hot, axis=0) - one_hot
    slots = jnp.sum(before * one_hot, axis=1)
    target = (flat_routes * capacity + slots).reshape(token_count, pick_count)
    places = jnp.arange(experts * capacity, dtype=jnp.int32)
    matched = target[:, :, None] == places[None, None, :]
    placing = jnp.transpose(jnp.any(matched, axis=1).astype(jnp.bfloat16))
    gate_weight = expert_gate[0]
    up_weight = expert_up[0]
    down_weight = expert_down[0]
    local_width = moe_input.shape[1]
    outgoing = jnp.dot(placing, moe_input, preferred_element_type=jnp.float32).astype(jnp.bfloat16)
    outgoing = outgoing.reshape(experts, capacity, local_width)
    arrived = lax.all_to_all(outgoing, "ep", split_axis=0, concat_axis=0, tiled=True)
    piece = lax.all_gather(arrived, "ctx", axis=2, tiled=True)
    slot_rows = piece.reshape(piece.shape[0] * piece.shape[1], piece.shape[2])
    gate_add = jnp.dot(slot_rows, gate_weight, preferred_element_type=jnp.float32)
    up_add = jnp.dot(slot_rows, up_weight, preferred_element_type=jnp.float32)
    hidden = (jax.nn.silu(gate_add) * up_add).astype(jnp.bfloat16)
    partial_out = jnp.dot(hidden, down_weight, preferred_element_type=jnp.float32).reshape(
        arrived.shape[0], capacity, -1
    )
    summed = lax.psum_scatter(
        partial_out.astype(jnp.bfloat16), "ctx", scatter_dimension=2, tiled=True
    ).astype(jnp.float32)
    returned = lax.all_to_all(
        summed.astype(jnp.bfloat16), "ep", split_axis=0, concat_axis=0, tiled=True
    ).astype(summed.dtype)
    flat_returned = returned.reshape(experts * capacity, returned.shape[2])
    picked_rows = flat_returned[target]
    routed = jnp.sum(picked_rows * route_gates[:, :, None], axis=1)
    return (moe_input.astype(jnp.float32) + routed).astype(jnp.bfloat16)


def solution(mesh):
    return jax.shard_map(
        local,
        mesh=mesh,
        in_specs=(
            P("ctx", "ep", None),
            P("ctx", None),
            P("ep", None, None),
            P("ep", "ctx"),
            P("ep", "ctx"),
            P("ep", None, "ctx"),
            P("ep", None, "ctx"),
            P("ep", "ctx", None),
            P("ep", None),
            P("ep", None),
        ),
        out_specs=P("ep", "ctx"),
        check_vma=False,
    )
```

profile of v0, /device:TPU:32, one launch (start us, length us, event | category | flops | bytes accessed | tf_op | source)
XLA Modules:
  0.0 666.4 jit_solution(14762429404576021311)
XLA Ops:
  6.5 0.7 all-gather.4.cloned.1.call-update
  7.3 0.1 broadcast_in_dim.10
  7.4 0.1 le.16
  7.5 53.8 %all-gather.4.cloned.1.call-done = bf16[4096,576]{0,1:T(8,128)(2,1)} async-done(((bf16[256,576]{0,1:T(8,128)(2,1)}), bf16[4096,576]{0,1:T(8,128)(2,1)}) %all-gather.4.cloned.1.call-update) | async-done | bytes 4718608 | tf_op jit(solution)/shard_map/all_gather | solution.py:34
  61.3 6.1 fusion.41
  67.5 1.3 fusion
  68.7 1.0 copy-done.7
  69.8 2.5 fusion.22
  72.3 0.4 fusion.33
  72.7 0.7 copy.66
  73.5 36.5 %all-gather.6.cloned.1.call-done = bf16[1024,1024]{1,0:T(8,128)(2,1)} async-done(((bf16[64,1024]{1,0:T(8,128)(2,1)}), bf16[1024,1024]{1,0:T(8,128)(2,1)}) %all-gather.6.cloned.1.call-update) | async-done | bytes 2097168 | tf_op jit(solution)/shard_map/all_gather | solution.py:52
  109.9 3.8 convolution_convert_fusion.1
  113.9 0.1 copy.47
  113.9 0.1 eq.42
  114.0 0.1 eq.38
  114.1 1.2 reduce-window.6
  115.3 0.2 slice_reduce_fusion
  115.6 0.1 fusion.39
  115.7 0.1 reduce_sum.31
  115.8 0.1 copy.51
  115.9 0.5 fusion.11
  116.4 83.3 %reduce-scatter.5.cloned.1.call-done = bf16[64,448]{1,0:T(8,128)(2,1)} async-done(((bf16[1024,448]{1,0:T(8,128)(2,1)}), bf16[64,448]{1,0:T(8,128)(2,1)}) %reduce-scatter.5.cloned.1.call-update) | async-done | bytes 57360 | tf_op jit(solution)/shard_map/reduce_scatter | solution.py:56
  199.7 1.2 convolution_convert_fusion.2
  200.9 0.2 copy.52
  201.2 0.1 reshape.59
  201.3 22.2 %all_to_all.10 = bf16[16,36,448]{2,1,0:T(8,128)(2,1)S(1)} all-to-all(bf16[16,36,448]{2,1,0:T(8,128)(2,1)S(1)} %reshape.59), channel_id=1, replica_groups=mesh['ctx'=16,'ep'=16] {'ep'}, dimensions={0} | all-to-all | bytes 1032192 | tf_op jit(solution)/shard_map/all_to_all | solution.py:81
  223.6 2.1 copy.53
  225.7 0.2 reduce-scatter.7.cloned.1.call-start
  225.9 152.6 %all-gather.8.cloned.1.call-done = bf16[16,36,7168]{1,0,2:T(8,128)(2,1)} async-done(((bf16[16,36,448]{1,0,2:T(8,128)(2,1)}), bf16[16,36,7168]{1,0,2:T(8,128)(2,1)}) %all-gather.8.cloned.1.call-update) | async-done | bytes 8257552 | tf_op jit(solution)/shard_map/all_gather | solution.py:82
  378.5 40.5 %reshape.76 = bf16[576,7168]{0,1:T(8,128)(2,1)} reshape(bf16[16,36,7168]{1,0,2:T(8,128)(2,1)} %all-gather.8.cloned.1.call-done) | data formatting | bytes 16515072 | tf_op jit(solution)/shard_map/reshape | solution.py:83
  419.0 6.8 %fusion.9 = f32[576,128]{1,0:T(8,128)S(1)} fusion(bf16[576,7168]{0,1:T(8,128)(2,1)} %reshape.76, bf16[1,7168,128]{2,1,0:T(8,128)(2,1)} %param.15), kind=kOutput, calls=%fused_computation.13 | convolution fusion | flops 1056964608 | bytes 10387456 | tf_op jit(solution)/shard_map/dot_general | solution.py:84
  425.9 0.4 copy-done.8
  426.3 2.7 fusion.30
  429.1 6.1 convolution_convert_fusion
  435.2 32.2 %copy.58 = bf16[16,36,7168]{1,0,2:T(8,128)(2,1)} copy(bf16[16,36,7168]{2,1,0:T(8,128)(2,1)} %convolution_convert_fusion) | data formatting | bytes 16515072
  467.4 40.5 %reshape.77 = bf16[7168,576]{1,0:T(8,128)(2,1)} reshape(bf16[7168,16,36]{2,1,0:T(8,128)(2,1)} %bitcast.62) | data formatting | bytes 16515072
  507.9 105.3 %reduce-scatter.7.cloned.1.call-done = bf16[448,576]{1,0:T(8,128)(2,1)} async-done(((bf16[7168,576]{1,0:T(8,128)(2,1)}), bf16[448,576]{1,0:T(8,128)(2,1)}) %reduce-scatter.7.cloned.1.call-update) | async-done | bytes 516112
  613.2 4.5 reshape.78
  617.7 3.4 copy.59
  621.1 10.3 %all-to-all-start.1 = ((bf16[16,36,448]{2,1,0:T(8,128)(2,1)}), bf16[16,36,448]{2,1,0:T(8,128)(2,1)}, u32[]{:S(2)}, u32[]{:S(2)}) async-start(bf16[16,36,448]{2,1,0:T(8,128)(2,1)} %copy.59), calls=%async_computation.2 | async-start | bytes 1310720 | tf_op jit(solution)/shard_map/all_to_all | solution.py:93
  631.4 0.1 copy.55
  631.5 0.1 reshape.67
  631.6 0.1 copy.56
  631.7 22.3 %all-to-all-done.1 = bf16[16,36,448]{2,1,0:T(8,128)(2,1)} async-done(((bf16[16,36,448]{2,1,0:T(8,128)(2,1)}), bf16[16,36,448]{2,1,0:T(8,128)(2,1)}, u32[]{:S(2)}, u32[]{:S(2)}) %all-to-all-start.1) | async-done | bytes 516128 | tf_op jit(solution)/shard_map/all_to_all | solution.py:93
  653.9 1.3 reshape.64
  655.3 2.3 gather_fusion
  657.6 1.6 fusion.34
  659.2 0.7 add_convert_fusion
  (35 shorter events, 0.4 us)
Async XLA Ops:
  6.5 422.5 %copy-start = (bf16[1,128,7168]{2,1,0:T(8,128)(2,1)S(1)}, bf16[1,128,7168]{2,1,0:T(8,128)(2,1)}, u32[]{:S(2)}) copy-start(bf16[1,128,7168]{2,1,0:T(8,128)(2,1)} %param.17) | copy-start | bytes 5505028
  6.5 54.8 %all-gather.4.cloned.1.call-start = ((), (), s32[]{:S(2)}) async-start(), calls=%async_computation.4 | async-start | bytes 5013504 | tf_op jit(solution)/shard_map/all_gather | solution.py:34
  7.3 102.7 %all-gather.6.cloned.1.call-start = ((), (), s32[]{:S(2)}) async-start(), calls=%async_computation.5 | async-start | bytes 2228224 | tf_op jit(solution)/shard_map/all_gather | solution.py:52
  67.4 2.3 copy-start.7
  69.8 2.5 copy-start.2
  69.8 40.1 %copy-start.9 = (bf16[1024,448]{0,1:T(8,128)(2,1)S(1)}, bf16[1024,448]{0,1:T(8,128)(2,1)}, u32[]{:S(2)}) copy-start(bf16[1024,448]{0,1:T(8,128)(2,1)} %param.13) | copy-start | bytes 2752516
  73.4 40.5 %copy-start.5 = (s32[64,8]{0,1:T(8,128)S(1)}, s32[64,8]{0,1:T(8,128)}, u32[]{:S(2)}) copy-start(s32[64,8]{0,1:T(8,128)} %param.18) | copy-start | bytes 6148
  73.4 126.3 %copy-start.3 = (bf16[64,448]{1,0:T(8,128)(2,1)S(1)}, bf16[64,448]{1,0:T(8,128)(2,1)}, u32[]{:S(2)}) copy-start(bf16[64,448]{1,0:T(8,128)(2,1)} %param.14) | copy-start | bytes 172036
  73.4 126.3 %reduce-scatter.5.cloned.1.call-start = ((), (), s32[]{:S(2)}) async-start(), calls=%async_computation.6 | async-start | bytes 1114112 | tf_op jit(solution)/shard_map/reduce_scatter | solution.py:56
  113.8 264.7 %all-gather.8.cloned.1.call-start = ((), (), s32[]{:S(2)}) async-start(), calls=%async_computation.7 | async-start | bytes 31195136 | tf_op jit(solution)/shard_map/all_gather | solution.py:82
  225.7 387.5 %reduce-scatter.7.cloned.1.call-start = ((), (), s32[]{:S(2)}) async-start(), calls=%async_computation.8 | async-start | bytes 9748480
  419.0 6.8 %copy-start.1 = (bf16[576,7168]{0,1:T(8,128)(2,1)S(1)}, bf16[576,7168]{0,1:T(8,128)(2,1)}, u32[]{:S(2)}) copy-start(bf16[576,7168]{0,1:T(8,128)(2,1)} %reshape.76) | copy-start | bytes 24772612
  419.0 7.2 %copy-start.8 = (bf16[1,7168,128]{2,1,0:T(8,128)(2,1)S(1)}, bf16[1,7168,128]{2,1,0:T(8,128)(2,1)}, u32[]{:S(2)}) copy-start(bf16[1,7168,128]{2,1,0:T(8,128)(2,1)} %param.16) | copy-start | bytes 5505028
  507.9 123.7 %copy-start.6 = (f32[64,8]{0,1:T(8,128)S(1)}, f32[64,8]{0,1:T(8,128)}, u32[]{:S(2)}) copy-start(f32[64,8]{0,1:T(8,128)} %param.19) | copy-start | bytes 6148
  621.1 32.8 %all-to-all-start.1 = ((bf16[16,36,448]{2,1,0:T(8,128)(2,1)}), bf16[16,36,448]{2,1,0:T(8,128)(2,1)}, u32[]{:S(2)}, u32[]{:S(2)}) async-start(bf16[16,36,448]{2,1,0:T(8,128)(2,1)} %copy.59), calls=%async_computation.2 | async-start | bytes 1310720 | tf_op jit(solution)/shard_map/all_to_all | solution.py:93
  655.3 3.9 copy-start.4
Sparse Core Ops, SparseCore 0:
  9.1 52.1 all-gather.3
  73.5 36.3 all-gather.5
  113.9 85.7 reduce-scatter.4
  225.8 152.6 all-gather.7
  508.0 105.1 reduce-scatter.6
where the time goes:
time: 670 us; the launch traced here: 666 us
  waiting for transfers between devices  455 us (68%)
  local copies, waits for them, and re-layouts  131 us (20%)
  matrix products  29.7 us (4%)
  blocking collectives  22.2 us (3%)
  between operations  13.4 us (2%)
  starting transfers between devices  10.6 us (2%)
    all_gather x1, waiting for transfers between devices, local(): piece = lax.all_gather(arrived, 'ctx', axis=2, tiled=True)  153 us
    unnamed x6, waiting for transfers between devices  106 us
    reduce_scatter x1, waiting for transfers between devices, local(): lax.psum_scatter(spread.astype(jnp.bfloat16), 'ep', scatter_dimension=0,...  83.3 us
    unnamed x26, local copies, waits for them, and re-layouts  82.3 us
    all_gather x1, waiting for transfers between devices, local(): piece = lax.all_gather(latents, 'ctx', axis=0, tiled=True)  53.8 us
    reshape x1, local copies, waits for them, and re-layouts, local(): slot_rows = piece.reshape(piece.shape[0] * piece.shape[1], piece.shape[2])  40.5 us
    all_gather x1, waiting for transfers between devices, local(): lax.all_gather(head_out, 'ctx', axis=0, tiled=True)  36.5 us
    all_to_all x1, waiting for transfers between devices, local(): lax.all_to_all(summed.astype(jnp.bfloat16), 'ep', split_axis=0, concat_ax...  22.3 us
  transfers between devices with their start and end apart: 6, of which 6 were waited for; matrix products, arithmetic and copies ran while one was open for 0% of the time, Pallas kernels for 0%

commit v1 on v0

--- a/solution.py
+++ b/solution.py
@@ -31,7 +31,9 @@
     row_pos = jnp.repeat(query_pos, head_count)
     query_rows = queries.reshape(query_count * head_count, feature_width)
     row_count = query_count * head_count
-    piece = lax.all_gather(latents, "ctx", axis=0, tiled=True)
+    padding = -feature_width % 128
+    query_rows = jnp.pad(query_rows, ((0, 0), (0, padding)))
+    piece = lax.all_gather(jnp.pad(latents, ((0, 0), (0, padding))), "ctx", axis=0, tiled=True)
     running_max = jnp.full((row_count,), NEG, jnp.float32)
     scores = jnp.einsum("qc,kc->qk", query_rows, piece, preferred_element_type=jnp.float32) * scale
     key_pos = jnp.arange(piece.shape[0], dtype=jnp.int32)
@@ -53,9 +55,14 @@
         out_proj,
         preferred_element_type=jnp.float32,
     )
-    attended = lax.psum_scatter(
-        spread.astype(jnp.bfloat16), "ep", scatter_dimension=0, tiled=True
-    ).astype(jnp.float32)
+    arrived = lax.all_to_all(
+        spread.astype(jnp.bfloat16).reshape(ep_devices, -1, spread.shape[1]),
+        "ep",
+        split_axis=0,
+        concat_axis=0,
+        tiled=True,
+    )
+    attended = jnp.sum(arrived.astype(jnp.float32), axis=0)
     moe_input = (residual.astype(jnp.float32) + attended).astype(jnp.bfloat16)
     token_count, pick_count = route_ids.shape
     experts = ep_devices * expert_gate.shape[0]
@@ -79,17 +86,20 @@
     outgoing = jnp.dot(placing, moe_input, preferred_element_type=jnp.float32).astype(jnp.bfloat16)
     outgoing = outgoing.reshape(experts, capacity, local_width)
     arrived = lax.all_to_all(outgoing, "ep", split_axis=0, concat_axis=0, tiled=True)
-    piece = lax.all_gather(arrived, "ctx", axis=2, tiled=True)
-    slot_rows = piece.reshape(piece.shape[0] * piece.shape[1], piece.shape[2])
-    gate_add = jnp.dot(slot_rows, gate_weight, preferred_element_type=jnp.float32)
-    up_add = jnp.dot(slot_rows, up_weight, preferred_element_type=jnp.float32)
+    slot_rows = lax.all_gather(arrived.reshape(-1, local_width), "ctx", axis=0)
+    gate_weight = gate_weight.reshape(ctx_devices, local_width, -1)
+    up_weight = up_weight.reshape(ctx_devices, local_width, -1)
+    gate_add = jnp.einsum("csf,cfh->sh", slot_rows, gate_weight, preferred_element_type=jnp.float32)
+    up_add = jnp.einsum("csf,cfh->sh", slot_rows, up_weight, preferred_element_type=jnp.float32)
     hidden = (jax.nn.silu(gate_add) * up_add).astype(jnp.bfloat16)
-    partial_out = jnp.dot(hidden, down_weight, preferred_element_type=jnp.float32).reshape(
-        arrived.shape[0], capacity, -1
+    hidden_width = hidden.shape[1]
+    down_blocks = jnp.transpose(
+        down_weight.reshape(hidden_width, ctx_devices, local_width), (1, 0, 2)
     )
-    summed = lax.psum_scatter(
-        partial_out.astype(jnp.bfloat16), "ctx", scatter_dimension=2, tiled=True
-    ).astype(jnp.float32)
+    down_blocks = lax.all_to_all(down_blocks, "ctx", split_axis=0, concat_axis=0, tiled=True)
+    hidden = lax.all_gather(hidden, "ctx", axis=0)
+    summed = jnp.einsum("csh,chf->sf", hidden, down_blocks, preferred_element_type=jnp.float32)
+    summed = summed.reshape(arrived.shape[0], capacity, local_width)
     returned = lax.all_to_all(
         summed.astype(jnp.bfloat16), "ep", split_axis=0, concat_axis=0, tiled=True
     ).astype(summed.dtype)

time: 670 us -> 344 us (0.51)
  waiting for transfers between devices: 455 us -> 199 us
  local copies, waits for them, and re-layouts: 131 us -> 17.1 us
  blocking collectives: 22.2 us -> 59.9 us
  starting transfers between devices: 10.6 us -> 17.6 us
    unnamed x6 -> x4, waiting for transfers between devices: 106 us -> 0.07 us
    all_gather x2 -> x3, waiting for transfers between devices: 206 us -> 121 us  [the longest x1 56 us: local(): slot_rows = lax.all_gather(arrived.reshape(-1, local_width), 'ctx', axis=0)]
    reduce_scatter x1 -> x0, waiting for transfers between devices: 83.3 us -> none  [local(): lax.psum_scatter(spread.astype(jnp.bfloat16), 'ep', scatter_dimension=0,...]
    unnamed x26 -> x19, local copies, waits for them, and re-layouts: 82.3 us -> 5.7 us
    reshape x1 -> x0, local copies, waits for them, and re-layouts: 40.5 us -> none  [local(): slot_rows = piece.reshape(piece.shape[0] * piece.shape[1], piece.shape[2])]
    all_to_all x0 -> x1, blocking collectives: none -> 35.2 us  [local(): lax.all_to_all(down_blocks, 'ctx', split_axis=0, concat_axis=0, tiled=True)]
    all_to_all x0 -> x1, waiting for transfers between devices: none -> 24.6 us  [local(): lax.all_to_all(spread.astype(jnp.bfloat16).reshape(ep_devices, -1, spread...]
    all_to_all x0 -> x1, starting transfers between devices: none -> 8.86 us  [local(): lax.all_to_all(spread.astype(jnp.bfloat16).reshape(ep_devices, -1, spread...]
  transfers between devices with their start and end apart: 6 -> 6, of which waited for: 6 -> 6; matrix products, arithmetic and copies ran while one was open for 0% -> 2% of each run, Pallas kernels for 0% -> 0%
where the time goes in v1:
time: 344 us; the launch traced here: 339 us
  waiting for transfers between devices  199 us (58%)
  blocking collectives  59.9 us (17%)
  matrix products  25.9 us (8%)
  starting transfers between devices  17.6 us (5%)
  local copies, waits for them, and re-layouts  17.1 us (5%)
  between operations  13.3 us (4%)
  other arithmetic  5.46 us (2%)
    all_gather x1, waiting for transfers between devices, local(): slot_rows = lax.all_gather(arrived.reshape(-1, local_width), 'ctx', axis=0)  56 us
    all_gather x1, waiting for transfers between devices, local(): lax.all_gather(jnp.pad(latents, ((0, 0), (0, padding))), 'ctx', axis=0, t...  54.6 us
    all_gather x1, waiting for transfers between devices, local(): lax.all_gather(head_out, 'ctx', axis=0, tiled=True)  35.9 us
    all_to_all x1, blocking collectives, local(): lax.all_to_all(down_blocks, 'ctx', split_axis=0, concat_axis=0, tiled=True)  35.2 us
    all_to_all x1, blocking collectives, local(): lax.all_to_all(outgoing, 'ep', split_axis=0, concat_axis=0, tiled=True)  24.6 us
    all_to_all x1, waiting for transfers between devices, local(): lax.all_to_all(spread.astype(jnp.bfloat16).reshape(ep_devices, -1, spread...  24.6 us
    all_to_all x1, waiting for transfers between devices, local(): lax.all_to_all(summed.astype(jnp.bfloat16), 'ep', split_axis=0, concat_ax...  17.4 us
    all_gather x1, waiting for transfers between devices, local(): hidden = lax.all_gather(hidden, 'ctx', axis=0)  10.5 us
  transfers between devices with their start and end apart: 6, of which 6 were waited for; matrix products, arithmetic and copies ran while one was open for 2% of the time, Pallas kernels for 0%

profile of v1, /device:TPU:32, one launch (start us, length us, event | category | flops | bytes accessed | tf_op | source)
XLA Modules:
  0.0 338.5 jit_solution(17634718911657428297)
XLA Ops:
  6.5 1.8 pad.9
  8.5 0.1 le.16
  8.6 54.6 %all-gather.6.cloned.1.call-done = bf16[4096,640]{0,1:T(8,128)(2,1)} async-done(((bf16[256,640]{0,1:T(8,128)(2,1)}), bf16[4096,640]{0,1:T(8,128)(2,1)}) %all-gather.6.cloned.1.call-update) | async-done | bytes 5242896 | tf_op jit(solution)/shard_map/all_gather | solution.py:36
  63.3 6.2 %fusion.34 = (f32[512]{0:T(512)S(1)}, f32[512,4096]{1,0:T(8,128)S(1)}) fusion(bf16[4096,640]{0,1:T(8,128)(2,1)} %all-gather.6.cloned.1.call-done, bf16[512,576]{1,0:T(8,128)(2,1)} %bitcast.68, s32[512]{0:T(512)S(1)} %le.16), kind=kOutput, calls=%fused_computation.47 | convolution fusion | flops 2692742656 | bytes 14225408 | tf_op jit(solution)/shard_map/qc,kc->qk/dot_general | solution.py:38
  69.5 1.3 fusion
  70.7 1.2 copy-done.6
  71.9 2.5 fusion.18
  74.4 0.4 fusion.25
  74.8 0.7 copy.75
  75.5 35.9 %all-gather.8.cloned.1.call-done = bf16[1024,1024]{1,0:T(8,128)(2,1)} async-done(((bf16[64,1024]{1,0:T(8,128)(2,1)}), bf16[1024,1024]{1,0:T(8,128)(2,1)}) %all-gather.8.cloned.1.call-update) | async-done | bytes 2097168 | tf_op jit(solution)/shard_map/all_gather | solution.py:54
  111.4 3.0 convolution_convert_fusion
  114.4 1.3 copy.57
  115.7 8.9 %all-to-all-start = ((bf16[16,64,448]{2,1,0:T(8,128)(2,1)}), bf16[16,64,448]{2,1,0:T(8,128)(2,1)S(1)}, u32[]{:S(2)}, u32[]{:S(2)}) async-start(bf16[16,64,448]{2,1,0:T(8,128)(2,1)} %bitcast.64), calls=%async_computation | async-start | bytes 2097152 | tf_op jit(solution)/shard_map/all_to_all | solution.py:58
  124.7 0.1 copy.58
  124.7 0.1 eq.42
  124.8 0.1 eq.38
  124.9 1.2 reduce-window.6
  126.1 0.2 slice_reduce_fusion
  126.3 0.1 fusion.31
  126.4 0.1 reduce_sum.41
  126.6 0.1 copy.62
  126.7 0.5 fusion.7
  127.2 24.6 %all-to-all-done = bf16[16,64,448]{2,1,0:T(8,128)(2,1)S(1)} async-done(((bf16[16,64,448]{2,1,0:T(8,128)(2,1)}), bf16[16,64,448]{2,1,0:T(8,128)(2,1)S(1)}, u32[]{:S(2)}, u32[]{:S(2)}) %all-to-all-start) | async-done | bytes 917536 | tf_op jit(solution)/shard_map/all_to_all | solution.py:58
  151.8 0.2 convert_reduce_fusion
  152.0 0.4 convolution_convert_fusion.1
  152.3 0.2 copy.63
  152.6 0.1 reshape.60
  152.7 24.6 %all_to_all.20 = bf16[16,36,448]{2,1,0:T(8,128)(2,1)S(1)} all-to-all(bf16[16,36,448]{2,1,0:T(8,128)(2,1)S(1)} %reshape.60), channel_id=1, replica_groups=mesh['ctx'=16,'ep'=16] {'ep'}, dimensions={0} | all-to-all | bytes 1032192 | tf_op jit(solution)/shard_map/all_to_all | solution.py:88
  177.4 0.2 all_gather_reshape.3
  177.6 1.1 copy.64
  178.7 0.2 all-gather.12.cloned.1.call-start
  179.0 56.0 %all-gather.10.cloned.1.call-done = bf16[16,576,448]{1,2,0:T(8,128)(2,1)} async-done(((bf16[1,576,448]{1,2,0:T(8,128)(2,1)}), bf16[16,576,448]{1,2,0:T(8,128)(2,1)}) %all-gather.10.cloned.1.call-update) | async-done | bytes 8257552 | tf_op jit(solution)/shard_map/all_gather | solution.py:89
  235.0 6.3 %convolution_bitcast_fusion.2 = f32[576,128]{1,0:T(8,128)S(1)} fusion(bf16[16,576,448]{1,2,0:T(8,128)(2,1)} %all-gather.10.cloned.1.call-done, bf16[16,448,128]{2,1,0:T(8,128)(2,1)S(1)} %bitcast.62), kind=kOutput, calls=%fused_computation.20 | convolution fusion | flops 1056964608 | bytes 10387456 | tf_op jit(solution)/shard_map/csf,cfh->sh/dot_general | solution.py:92
  241.3 0.4 copy-done.7
  241.7 3.4 %fusion.24 = bf16[576,128]{1,0:T(8,128)(2,1)} fusion(bf16[16,576,448]{1,2,0:T(8,128)(2,1)S(1)} %copy-done.5, bf16[16,448,128]{2,1,0:T(8,128)(2,1)S(1)} %bitcast.67, f32[576,128]{1,0:T(8,128)S(1)} %convolution_bitcast_fusion.2), kind=kOutput, calls=%fused_computation.22 | convolution fusion | flops 1057406976 | bytes 10534912 | tf_op jit(solution)/shard_map/csf,cfh->sh/dot_general | solution.py:93
  245.1 3.9 %copy.65 = bf16[1,128,7168]{1,2,0:T(8,128)(2,1)} copy(bf16[1,128,7168]{2,1,0:T(8,128)(2,1)} %param.17) | data formatting | bytes 3670016 | tf_op args[7]
  249.1 35.2 %all_to_all.21 = bf16[16,128,448]{1,2,0:T(8,128)(2,1)} all-to-all(bf16[16,128,448]{1,2,0:T(8,128)(2,1)} %bitcast.63), channel_id=1, replica_groups=mesh['ctx'=16,'ep'=16] {'ctx'}, dimensions={0} | all-to-all | bytes 3670016 | tf_op jit(solution)/shard_map/all_to_all | solution.py:99
  284.3 10.5 %all-gather.12.cloned.1.call-done = bf16[9216,128]{1,0:T(8,128)(2,1)} async-done(((bf16[576,128]{1,0:T(8,128)(2,1)}), bf16[9216,128]{1,0:T(8,128)(2,1)}) %all-gather.12.cloned.1.call-update) | async-done | bytes 2359312 | tf_op jit(solution)/shard_map/all_gather | solution.py:100
  294.8 3.8 %fusion.6 = bf16[576,448]{0,1:T(8,128)(2,1)S(1)} fusion(bf16[16,576,128]{2,1,0:T(8,128)(2,1)} %bitcast.66, bf16[16,128,448]{1,2,0:T(8,128)(2,1)} %all_to_all.21), kind=kOutput, calls=%fused_computation.12 | convolution fusion | flops 1057222656 | bytes 4710400 | tf_op jit(solution)/shard_map/csh,chf->sf/dot_general | solution.py:101
  298.6 0.2 copy.66
  298.9 1.0 convert_element_type.69
  299.9 8.5 %all-to-all-start.3 = ((bf16[16,36,448]{2,1,0:T(8,128)(2,1)}), bf16[16,36,448]{2,1,0:T(8,128)(2,1)}, u32[]{:S(2)}, u32[]{:S(2)}) async-start(bf16[16,36,448]{2,1,0:T(8,128)(2,1)} %convert_element_type.69), calls=%async_computation.3 | async-start | bytes 1310720 | tf_op jit(solution)/shard_map/all_to_all | solution.py:103
  308.4 0.1 reshape.67
  308.6 17.4 %all-to-all-done.3 = bf16[16,36,448]{2,1,0:T(8,128)(2,1)} async-done(((bf16[16,36,448]{2,1,0:T(8,128)(2,1)}), bf16[16,36,448]{2,1,0:T(8,128)(2,1)}, u32[]{:S(2)}, u32[]{:S(2)}) %all-to-all-start.3) | async-done | bytes 516128 | tf_op jit(solution)/shard_map/all_to_all | solution.py:103
  326.1 1.3 reshape.64
  327.4 2.3 gather_fusion
  329.7 1.6 fusion.26
  331.3 0.7 add_convert_fusion
  (32 shorter events, 0.6 us)
Async XLA Ops:
  6.5 228.5 %copy-start = (bf16[1,7168,128]{2,1,0:T(8,128)(2,1)S(1)}, bf16[1,7168,128]{2,1,0:T(8,128)(2,1)}, u32[]{:S(2)}) copy-start(bf16[1,7168,128]{2,1,0:T(8,128)(2,1)} %param.15) | copy-start | bytes 5505028
  6.5 56.7 %all-gather.6.cloned.1.call-start = ((), (), s32[]{:S(2)}) async-start(), calls=%async_computation.4 | async-start | bytes 5570560 | tf_op jit(solution)/shard_map/all_gather | solution.py:36
  8.4 103.0 %all-gather.8.cloned.1.call-start = ((), (), s32[]{:S(2)}) async-start(), calls=%async_computation.5 | async-start | bytes 2228224 | tf_op jit(solution)/shard_map/all_gather | solution.py:54
  69.4 2.5 copy-start.6
  71.9 2.5 copy-start.1
  75.5 49.1 %copy-start.3 = (s32[64,8]{0,1:T(8,128)S(1)}, s32[64,8]{0,1:T(8,128)}, u32[]{:S(2)}) copy-start(s32[64,8]{0,1:T(8,128)} %param.18) | copy-start | bytes 6148
  114.4 37.6 %copy-start.2 = (bf16[64,448]{1,0:T(8,128)(2,1)S(1)}, bf16[64,448]{1,0:T(8,128)(2,1)}, u32[]{:S(2)}) copy-start(bf16[64,448]{1,0:T(8,128)(2,1)} %param.14) | copy-start | bytes 172036
  115.7 36.1 %all-to-all-start = ((bf16[16,64,448]{2,1,0:T(8,128)(2,1)}), bf16[16,64,448]{2,1,0:T(8,128)(2,1)S(1)}, u32[]{:S(2)}, u32[]{:S(2)}) async-start(bf16[16,64,448]{2,1,0:T(8,128)(2,1)} %bitcast.64), calls=%async_computation | async-start | bytes 2097152 | tf_op jit(solution)/shard_map/all_to_all | solution.py:58
  124.6 110.4 %all-gather.10.cloned.1.call-start = ((), (), s32[]{:S(2)}) async-start(), calls=%async_computation.6 | async-start | bytes 9748480 | tf_op jit(solution)/shard_map/all_gather | solution.py:89
  178.7 116.1 %all-gather.12.cloned.1.call-start = ((), (), s32[]{:S(2)}) async-start(), calls=%async_computation.7 | async-start | bytes 2506752 | tf_op jit(solution)/shard_map/all_gather | solution.py:100
  235.0 6.3 %copy-start.5 = (bf16[16,576,448]{1,2,0:T(8,128)(2,1)S(1)}, bf16[16,576,448]{1,2,0:T(8,128)(2,1)}, u32[]{:S(2)}) copy-start(bf16[16,576,448]{1,2,0:T(8,128)(2,1)} %all-gather.10.cloned.1.call-done) | copy-start | bytes 24772612
  235.0 6.7 %copy-start.7 = (bf16[1,7168,128]{2,1,0:T(8,128)(2,1)S(1)}, bf16[1,7168,128]{2,1,0:T(8,128)(2,1)}, u32[]{:S(2)}) copy-start(bf16[1,7168,128]{2,1,0:T(8,128)(2,1)} %param.16) | copy-start | bytes 5505028
  294.8 13.8 %copy-start.4 = (f32[64,8]{0,1:T(8,128)S(1)}, f32[64,8]{0,1:T(8,128)}, u32[]{:S(2)}) copy-start(f32[64,8]{0,1:T(8,128)} %param.19) | copy-start | bytes 6148
  299.9 26.2 %all-to-all-start.3 = ((bf16[16,36,448]{2,1,0:T(8,128)(2,1)}), bf16[16,36,448]{2,1,0:T(8,128)(2,1)}, u32[]{:S(2)}, u32[]{:S(2)}) async-start(bf16[16,36,448]{2,1,0:T(8,128)(2,1)} %convert_element_type.69), calls=%async_computation.3 | async-start | bytes 1310720 | tf_op jit(solution)/shard_map/all_to_all | solution.py:103
Sparse Core Ops, SparseCore 0:
  9.1 54.0 all-gather.5
  75.7 35.7 all-gather.7
  178.8 56.1 all-gather.9
  245.3 49.4 all-gather.11
